TPU v7x, 32 devices: a whole 2x2x4 slice. The times are simulated.
32 devices in a mesh: tensor: 4 (over y, core), dp: 8 (over z, x).
Axes of the slice: x: 2, y: 2, z: 4, core: 2. Of those that a mesh axis runs over, the one named last changes fastest.
Arguments:
- inputs: bfloat16 [4096, 512], P('dp'), may hold values from -6 to 6
- norm_gains: bfloat16 [5, 512], replicated, may hold values from 0.25 to 1.75
- early_up: bfloat16 [512, 2048], P(None, 'tensor'), may hold values from -0.25 to 0.25
- early_down: bfloat16 [2048, 512], P('tensor'), may hold values from -0.25 to 0.25
- query_key_value: bfloat16 [512, 3, 512], P(None, None, 'tensor'), may hold values from -0.25 to 0.25
- position_weight: bfloat16 [512, 512], P(None, 'tensor'), may hold values from -0.25 to 0.25
- position_bias: bfloat16 [2, 8, 64], P(None, 'tensor'), may hold values from -3 to 3
- attention_out: bfloat16 [512, 512], P('tensor'), may hold values from -0.75 to 0.75
- pointwise_in: bfloat16 [512, 2, 512], P(None, None, 'tensor'), may hold values from -0.25 to 0.25
- depthwise: bfloat16 [31, 512], P(None, 'tensor'), may hold values from -1 to 1
- batch_gain: bfloat16 [512], P('tensor'), may hold values from 0.25 to 1.75
- batch_bias: bfloat16 [512], P('tensor'), may hold values from -3 to 3
- pointwise_out: bfloat16 [512, 512], P('tensor'), may hold values from -0.375 to 0.375
- late_up: bfloat16 [512, 2048], P(None, 'tensor'), may hold values from -0.25 to 0.25
- late_down: bfloat16 [2048, 512], P('tensor'), may hold values from -0.25 to 0.25
- output_cotangent: bfloat16 [4096, 512], P('dp'), may hold values from -6 to 6
Outputs:
- layer_output: bfloat16 [4096, 512], P('dp')
- input_gradient: float32 [4096, 512], P('dp')
- gains_gradient: float32 [5, 512], replicated
- early_up_gradient: float32 [512, 2048], P(None, 'tensor')
- early_down_gradient: float32 [2048, 512], P('tensor')
- query_key_value_gradient: float32 [512, 3, 512], P(None, None, 'tensor')
- position_weight_gradient: float32 [512, 512], P(None, 'tensor')
- position_bias_gradient: float32 [2, 8, 64], P(None, 'tensor')
- attention_out_gradient: float32 [512, 512], P('tensor')
- pointwise_in_gradient: float32 [512, 2, 512], P(None, None, 'tensor')
- depthwise_gradient: float32 [31, 512], P(None, 'tensor')
- batch_gain_gradient: float32 [512], P('tensor')
- batch_bias_gradient: float32 [512], P('tensor')
- pointwise_out_gradient: float32 [512, 512], P('tensor')
- late_up_gradient: float32 [512, 2048], P(None, 'tensor')
- late_down_gradient: float32 [2048, 512], P('tensor')
All inputs are finite; a program needn't handle non-finite values.
Results may differ from a plain program's by a relative error of at most 0.02.
Values sent between devices are 32-bit elements; how exact they have to be, the bound alone decides.
A program may use at most 128 MiB of HBM per device.

v0:
```python
import math
import jax
import jax.numpy as jnp
from jax import lax
from jax.sharding import PartitionSpec as P

LENGTH = 512
EPS = 1e-05


def plain_round(v):
    return lax.optimization_barrier(v.astype(jnp.bfloat16)).astype(jnp.float32)


def plain_same(v):
    return v


def value_keep(v):
    return (plain_round(v), None)


def value_pass(kept, grad):
    return (grad,)


def grad_keep(v):
    return (v, None)


def grad_round(kept, grad):
    return (plain_round(grad),)


def low(v):
    rounder = jax.custom_vjp(plain_round)
    rounder.defvjp(value_keep, value_pass)
    return rounder(v)


def low_back(v):
    rounder = jax.custom_vjp(plain_same)
    rounder.defvjp(grad_keep, grad_round)
    return rounder(v)


def matmul(first_factor, second_factor):
    return jnp.dot(first_factor, second_factor, preferred_element_type=jnp.float32)


def layer_norm(values, gain_row):
    centre = values - jnp.mean(values, axis=-1, keepdims=True)
    spread = jnp.mean(centre * centre, axis=-1, keepdims=True)
    return centre * lax.rsqrt(spread + EPS) * gain_row


def sinusoid_table(length, model_width):
    offsets = (length - 1 - jnp.arange(2 * length - 1)).astype(jnp.float32)
    frequency = jnp.exp(
        jnp.arange(0, model_width, 2).astype(jnp.float32) * (-math.log(10000.0) / model_width)
    )
    phases = offsets[:, None] * frequency[None, :]
    return jnp.stack([jnp.sin(phases), jnp.cos(phases)], axis=-1).reshape(
        2 * length - 1, model_width
    )


def relative_shift(scores):
    head_count, length, span_size = scores.shape
    padded = jnp.pad(scores, ((0, 0), (0, 0), (1, 0)))
    padded = padded.reshape(head_count, 2 * length, length)[:, 1:]
    return padded.reshape(head_count, length, span_size)[:, :, :length]


def feed_forward(values, gain_row, weight_in, weight_out):
    normed = low(layer_norm(values, gain_row))
    hidden = low_back(matmul(normed, weight_in))
    active = low(jax.nn.silu(hidden))
    return low_back(matmul(active, weight_out))


def sequence_core(sequence, sinusoid, weight_pos, biases):
    length = sequence.shape[0]
    head_count = sequence.shape[2]
    head_size = sequence.shape[3]
    queries = sequence[:, 0]
    key_rows = low(sequence[:, 1])
    values = low(sequence[:, 2])
    position = low(low_back(matmul(sinusoid, weight_pos))).reshape(
        2 * length - 1, head_count, head_size
    )
    with_content = low(queries + biases[0])
    with_position = low(queries + biases[1])
    content = jnp.einsum("ihd,jhd->hij", with_content, key_rows, preferred_element_type=jnp.float32)
    relative = relative_shift(
        jnp.einsum("ihd,rhd->hir", with_position, position, preferred_element_type=jnp.float32)
    )
    scores = low_back((content + relative) * (1.0 / math.sqrt(head_size)))
    weights = low(jax.nn.softmax(scores, axis=-1))
    return jnp.einsum("hij,jhd->ihd", weights, values, preferred_element_type=jnp.float32)


def attention(values, gain_row, weight_qkv, weight_pos, biases, weight_out):
    model_width = weight_qkv.shape[0]
    local_width = weight_qkv.shape[2]
    head_count = biases.shape[1]
    head_size = biases.shape[2]
    normed = low(layer_norm(values, gain_row))
    mixed_rows = low_back(matmul(normed, weight_qkv.reshape(model_width, 3 * local_width)))
    mixed_rows = mixed_rows.reshape(-1, LENGTH, 3, head_count, head_size)
    sinusoid = low(sinusoid_table(LENGTH, model_width))
    per_sequence = jax.checkpoint(
        lambda sequence: sequence_core(sequence, sinusoid, weight_pos, biases)
    )
    attended = lax.map(per_sequence, mixed_rows).reshape(-1, local_width)
    attended = low(low_back(attended))
    return low_back(matmul(attended, weight_out))


def depthwise_conv(gated, kernel):
    half = kernel.shape[0] // 2
    return lax.conv_general_dilated(
        gated,
        kernel[:, None, :],
        (1,),
        [(half, half)],
        dimension_numbers=("NWC", "WIO", "NWC"),
        feature_group_count=gated.shape[2],
        precision=lax.Precision.HIGHEST,
    )


def conv_front(values, gain_row, weight_in, kernel):
    channels = kernel.shape[1]
    normed = low(layer_norm(values, gain_row))
    paired = low_back(matmul(normed, weight_in.reshape(weight_in.shape[0], 2 * channels))).reshape(
        -1, 2, channels
    )
    gated = paired[:, 0] * jax.nn.sigmoid(paired[:, 1])
    return depthwise_conv(gated.reshape(-1, LENGTH, channels), kernel)


def conv_back(mixed_rows, batch_mean, batch_var, scale_row, shift_row, weight_out):
    scaled = (mixed_rows - batch_mean) * lax.rsqrt(batch_var + EPS) * scale_row + shift_row
    swished = low(jax.nn.silu(scaled)).reshape(-1, mixed_rows.shape[2])
    return low_back(matmul(swished, weight_out))


def add_branch(base_rows, partial_value, factor):
    return base_rows + factor * lax.psum(partial_value, "tensor")


def add_gradient(base_rows, cotangent_in, gain_piece):
    cotangent_sum, gain_total = lax.psum((cotangent_in, gain_piece), "tensor")
    return (base_rows + cotangent_sum, gain_total)


def per_device(
    inputs,
    norm_gains,
    early_up,
    early_down,
    query_key_value,
    position_weight,
    position_bias,
    attention_out,
    pointwise_in,
    depthwise,
    batch_gain,
    batch_bias,
    pointwise_out,
    late_up,
    late_down,
    output_cotangent,
):
    stream = inputs.astype(jnp.float32)
    gain_rows = norm_gains.astype(jnp.float32)
    early_in = early_up.astype(jnp.float32)
    early_back = early_down.astype(jnp.float32)
    project_qkv = query_key_value.astype(jnp.float32)
    project_pos = position_weight.astype(jnp.float32)
    query_bias = position_bias.astype(jnp.float32)
    project_out = attention_out.astype(jnp.float32)
    point_first = pointwise_in.astype(jnp.float32)
    depth_taps = depthwise.astype(jnp.float32)
    scale_row = batch_gain.astype(jnp.float32)
    shift_row = batch_bias.astype(jnp.float32)
    point_second = pointwise_out.astype(jnp.float32)
    late_in = late_up.astype(jnp.float32)
    late_back = late_down.astype(jnp.float32)
    first_part, first_pull = jax.vjp(feed_forward, stream, gain_rows[0], early_in, early_back)
    after_first = add_branch(stream, first_part, 0.5)
    second_part, second_pull = jax.vjp(
        attention, after_first, gain_rows[1], project_qkv, project_pos, query_bias, project_out
    )
    after_second = add_branch(after_first, second_part, 1.0)
    mixed_rows, front_pull = jax.vjp(
        conv_front, after_second, gain_rows[2], point_first, depth_taps
    )
    token_count = mixed_rows.shape[0] * mixed_rows.shape[1] * lax.axis_size("dp")
    sum_values, sum_squares = lax.psum(
        (jnp.sum(mixed_rows, axis=(0, 1)), jnp.sum(mixed_rows * mixed_rows, axis=(0, 1))), "dp"
    )
    batch_mean = sum_values / token_count
    batch_var = sum_squares / token_count - batch_mean * batch_mean
    third_part, back_pull = jax.vjp(
        conv_back, mixed_rows, batch_mean, batch_var, scale_row, shift_row, point_second
    )
    after_third = add_branch(after_second, third_part, 1.0)
    fourth_part, fourth_pull = jax.vjp(feed_forward, after_third, gain_rows[3], late_in, late_back)
    after_fourth = add_branch(after_third, fourth_part, 0.5)
    result, final_pull = jax.vjp(layer_norm, after_fourth, gain_rows[4])
    grad_four, final_gain = final_pull(output_cotangent.astype(jnp.float32))
    cotangent_in, gain_piece, late_in_grad, late_back_grad = fourth_pull(0.5 * grad_four)
    grad_three, gain_four = add_gradient(grad_four, cotangent_in, gain_piece)
    final_gain, gain_four, late_in_grad, late_back_grad = (
        final_gain,
        gain_four,
        late_in_grad,
        late_back_grad,
    )
    direct_grad, mean_grad, var_grad, scale_grad, shift_grad, second_point_grad = back_pull(
        grad_three
    )
    mean_grad, var_grad = lax.psum((mean_grad, var_grad), "dp")
    mixed_grad = (
        direct_grad + (mean_grad + 2.0 * var_grad * (mixed_rows - batch_mean)) / token_count
    )
    cotangent_in, gain_piece, first_point_grad, depth_grad = front_pull(mixed_grad)
    grad_two, gain_two = add_gradient(grad_three, cotangent_in, gain_piece)
    gain_two, scale_grad, shift_grad, second_point_grad, first_point_grad, depth_grad = (
        gain_two,
        scale_grad,
        shift_grad,
        second_point_grad,
        first_point_grad,
        depth_grad,
    )
    cotangent_in, gain_piece, qkv_grad, pos_grad, bias_grad, out_grad = second_pull(grad_two)
    grad_one, gain_one = add_gradient(grad_two, cotangent_in, gain_piece)
    gain_one, qkv_grad, pos_grad, bias_grad, out_grad = (
        gain_one,
        qkv_grad,
        pos_grad,
        bias_grad,
        out_grad,
    )
    cotangent_in, gain_piece, early_in_grad, early_back_grad = first_pull(0.5 * grad_one)
    grad_zero, gain_zero = add_gradient(grad_one, cotangent_in, gain_piece)
    gain_zero, early_in_grad, early_back_grad = (gain_zero, early_in_grad, early_back_grad)
    gain_grads = jnp.stack([gain_zero, gain_one, gain_two, gain_four, final_gain])
    (
        gain_grads,
        early_in_grad,
        early_back_grad,
        qkv_grad,
        pos_grad,
        bias_grad,
        out_grad,
        first_point_grad,
        depth_grad,
        scale_grad,
        shift_grad,
        second_point_grad,
        late_in_grad,
        late_back_grad,
    ) = lax.psum(
        (
            gain_grads,
            early_in_grad,
            early_back_grad,
            qkv_grad,
            pos_grad,
            bias_grad,
            out_grad,
            first_point_grad,
            depth_grad,
            scale_grad,
            shift_grad,
            second_point_grad,
            late_in_grad,
            late_back_grad,
        ),
        "dp",
    )
    return (
        result.astype(jnp.bfloat16),
        grad_zero,
        gain_grads,
        early_in_grad,
        early_back_grad,
        qkv_grad,
        pos_grad,
        bias_grad,
        out_grad,
        first_point_grad,
        depth_grad,
        scale_grad,
        shift_grad,
        second_point_grad,
        late_in_grad,
        late_back_grad,
    )


def solution(mesh):
    return jax.shard_map(
        per_device,
        mesh=mesh,
        in_specs=(
            P("dp", None),
            P(),
            P(None, "tensor"),
            P("tensor", None),
            P(None, None, "tensor"),
            P(None, "tensor"),
            P(None, "tensor", None),
            P("tensor", None),
            P(None, None, "tensor"),
            P(None, "tensor"),
            P("tensor"),
            P("tensor"),
            P("tensor", None),
            P(None, "tensor"),
            P("tensor", None),
            P("dp", None),
        ),
        out_specs=(
            P("dp", None),
            P("dp", None),
            P(),
            P(None, "tensor"),
            P("tensor", None),
            P(None, None, "tensor"),
            P(None, "tensor"),
            P(None, "tensor", None),
            P("tensor", None),
            P(None, None, "tensor"),
            P(None, "tensor"),
            P("tensor"),
            P("tensor"),
            P("tensor", None),
            P(None, "tensor"),
            P("tensor", None),
        ),
        check_vma=False,
    )
```

profile of v0, /device:TPU:0, one launch (start us, length us, event | category | flops | bytes accessed | tf_op | source)
XLA Modules:
  0.0 733.0 jit_solution(10238060074771365690)
XLA Ops:
  17.1 31.0 %fusion.20 = (bf16[1023,256,1]{0,2,1:T(2,128)(2,1)S(1)}, bf16[1023,256,1]{0,2,1:T(2,128)(2,1)S(1)}) fusion(f32[1023]{0:T(1024)S(1)} %subtract_convert_fusion, f32[256]{0:T(256)S(1)} %multiply_exponential_fusion), kind=kLoop, calls=%fused_computation.49 | loop fusion | flops 785664 | bytes 1052668 | tf_op jit(solution)/shard_map/convert.3
  48.1 2.5 pad_maximum_fusion
  59.9 3.2 pad.50
  63.1 5.0 reshape.456
  68.1 4.9 slice.118
  73.0 6.5 reshape.457
  79.5 3.1 slice.119
  82.6 2.9 copy.109
  85.5 3.8 fusion.102
  94.2 37.0 %all-reduce.28.cloned.1.call-done = f32[512,512]{1,0:T(8,128)} async-done(((f32[512,512]{1,0:T(8,128)}), f32[512,512]{1,0:T(8,128)}) %all-reduce.28.cloned.1.call-update) | async-done | bytes 1048592 | tf_op jit(solution)/shard_map/psum | solution.py:150
  134.6 21.5 %all-reduce.13 = (f32[128]{0:T(128)S(1)}, f32[128]{0:T(128)S(1)}) all-reduce(f32[128]{0:T(128)S(1)} %get-tuple-element.85, f32[128]{0:T(128)S(1)} %get-tuple-element.84), channel_id=1, replica_groups=mesh['tensor'=4,'dp'=8] {'dp'}, use_global_device_ids=true, to_apply=%region_11.12 | all-reduce | flops 256 | bytes 2048 | tf_op jit(solution)/shard_map/psum | solution.py:201
  159.8 32.9 %all-reduce.30.cloned.1.call-done = f32[512,512]{1,0:T(8,128)} async-done(((f32[512,512]{1,0:T(8,128)}), f32[512,512]{1,0:T(8,128)}) %all-reduce.30.cloned.1.call-update) | async-done | bytes 1048592 | tf_op jit(solution)/shard_map/psum | solution.py:150
  199.7 36.5 %all-reduce.32.cloned.1.call-done = f32[512,512]{1,0:T(8,128)} async-done(((f32[512,512]{1,0:T(8,128)}), f32[512,512]{1,0:T(8,128)}) %all-reduce.32.cloned.1.call-update) | async-done | bytes 1048592 | tf_op jit(solution)/shard_map/psum | solution.py:150
  253.0 2.5 fusion.117
  255.5 25.7 %all-reduce.34.cloned.1.call-done = f32[512,512]{1,0:T(8,128)} async-done(((f32[512,512]{1,0:T(8,128)}), f32[512,512]{1,0:T(8,128)}) %all-reduce.34.cloned.1.call-update) | async-done | bytes 1048592 | tf_op jit(solution)/shard_map/psum | solution.py:154
  285.5 22.0 %all-reduce.12 = (f32[128]{0:T(128)}, f32[128]{0:T(128)}) all-reduce(f32[128]{0:T(128)} %neg.55, f32[128]{0:T(128)} %multiply_multiply_fusion.5), channel_id=1, replica_groups=mesh['tensor'=4,'dp'=8] {'dp'}, use_global_device_ids=true, to_apply=%region_26.27 | all-reduce | flops 256 | bytes 2048 | tf_op jit(solution)/shard_map/psum | solution.py:225
  320.7 2.7 fusion.116
  327.5 25.9 %all-reduce.36.cloned.1.call-done = f32[512,512]{1,0:T(8,128)} async-done(((f32[512,512]{1,0:T(8,128)}), f32[512,512]{1,0:T(8,128)}) %all-reduce.36.cloned.1.call-update) | async-done | bytes 1048592 | tf_op jit(solution)/shard_map/psum | solution.py:154
  353.4 2.7 fusion.89
  362.4 3.2 pad.53
  365.6 5.0 reshape.463
  370.5 4.9 slice.135
  375.4 6.5 reshape.464
  385.4 2.7 fusion.103
  396.1 6.1 reshape.465
  404.1 2.9 reshape.466
  419.0 30.1 %all-reduce.38.cloned.1.call-done = f32[512,512]{1,0:T(8,128)} async-done(((f32[512,512]{1,0:T(8,128)}), f32[512,512]{1,0:T(8,128)}) %all-reduce.38.cloned.1.call-update) | async-done | bytes 1048592 | tf_op jit(solution)/shard_map/psum | solution.py:154
  458.8 5.9 fusion.106
  464.7 6.3 all-reduce.15
  471.1 38.5 %all-reduce.11 = (f32[5,512]{1,0:T(8,128)}, f32[2,2,64]{2,1,0:T(2,128)}, f32[31,128]{1,0:T(8,128)}, f32[128]{0:T(128)}, f32[128]{0:T(128)}) all-reduce(f32[5,512]{1,0:T(8,128)S(1)} %stack.27, f32[2,2,64]{2,1,0:T(2,128)S(1)} %pad_add_fusion, f32[31,128]{1,0:T(8,128)S(1)} %bitcast.232, ...), channel_id=1, replica_groups=mesh['tensor'=4,'dp'=8] {'dp'}, use_global_device_ids=true, to_apply=%region_50.51 | all-reduce | flops 7040 | bytes 56320 | tf_op jit(solution)/shard_map/psum | solution.py:267
  509.6 2.4 add.310
  512.0 204.9 %all-reduce.42.cloned.1.call-done = (f32[512,512]{1,0:T(8,128)}, f32[512,512]{1,0:T(8,128)}, f32[512,3,128]{2,0,1:T(8,128)}, f32[512,128]{1,0:T(8,128)}, f32[128...) async-done(((f32[512,512]{1,0:T(8,128)}, f32[512,512]{1,0:T(8,128)}, f32[512,3,128]{2,0,1:T(8,128)}, ...) | async-done | bytes 6291472 | tf_op jit(solution)/shard_map/psum | solution.py:267
  (457 shorter events, 125.5 us)
Async XLA Ops:
  7.2 188.7 %copy-start = (bf16[512,512]{1,0:T(8,128)(2,1)S(1)}, bf16[512,512]{1,0:T(8,128)(2,1)}, u32[]{:S(2)}) copy-start(bf16[512,512]{1,0:T(8,128)(2,1)} %param.29) | copy-start | bytes 1572868
  7.2 6.1 copy-start.70
  7.2 48.8 %all-reduce.26.cloned.1.call-start = ((), (), s32[]{:S(2)}) async-start(), calls=%async_computation | async-start | bytes 2097152 | tf_op jit(solution)/shard_map/psum | solution.py:150
  8.6 6.2 copy-start.79
  12.0 45.8 %copy-start.110 = (f32[1,512]{1,0:T(1,128)}, f32[1,512]{1,0:T(1,128)S(1)}, u32[]{:S(2)}) copy-start(f32[1,512]{1,0:T(1,128)S(1)} %get-tuple-element.159) | copy-start | bytes 6148
  12.0 120.9 %copy-start.93 = (f32[1,512]{1,0:T(1,128)}, f32[1,512]{1,0:T(1,128)S(1)}, u32[]{:S(2)}) copy-start(f32[1,512]{1,0:T(1,128)S(1)} %get-tuple-element.158) | copy-start | bytes 6148
  17.0 114.1 %all-reduce.28.cloned.1.call-start = ((), (), s32[]{:S(2)}) async-start(), calls=%async_computation.1 | async-start | bytes 2097152 | tf_op jit(solution)/shard_map/psum | solution.py:150
  50.8 7.5 %copy-start.38 = (bf16[512,3,128]{0,2,1:T(8,128)(2,1)}, bf16[512,3,128]{0,2,1:T(8,128)(2,1)S(1)}, u32[]{:S(2)}) copy-start(bf16[512,3,128]{0,2,1:T(8,128)(2,1)S(1)} %copy.60) | copy-start | bytes 1179652
  51.7 5.8 copy-start.5
  57.4 73.7 %copy-start.2 = (f32[512,512]{1,0:T(8,128)}, f32[512,512]{1,0:T(8,128)S(1)}, u32[]{:S(2)}) copy-start(f32[512,512]{1,0:T(8,128)S(1)} %get-tuple-element.137) | copy-start | bytes 3145732
  93.5 99.2 %all-reduce.30.cloned.1.call-start = ((), (), s32[]{:S(2)}) async-start(), calls=%async_computation.2 | async-start | bytes 2097152 | tf_op jit(solution)/shard_map/psum | solution.py:150
  94.0 62.7 %copy-start.120 = (f32[128]{0:T(128)}, f32[128]{0:T(128)S(1)}, u32[]{:S(2)}) copy-start(f32[128]{0:T(128)S(1)} %convert_element_type.256) | copy-start | bytes 1540
  134.6 23.8 %copy-start.57 = (bf16[128,512]{1,0:T(8,128)(2,1)S(1)}, bf16[128,512]{1,0:T(8,128)(2,1)}, u32[]{:S(2)}) copy-start(bf16[128,512]{1,0:T(8,128)(2,1)} %param.28) | copy-start | bytes 393220
  159.8 76.5 %all-reduce.32.cloned.1.call-start = ((), (), s32[]{:S(2)}) async-start(), calls=%async_computation.3 | async-start | bytes 2097152 | tf_op jit(solution)/shard_map/psum | solution.py:150
  199.6 81.6 %all-reduce.34.cloned.1.call-start = ((), (), s32[]{:S(2)}) async-start(), calls=%async_computation.4 | async-start | bytes 2097152 | tf_op jit(solution)/shard_map/psum | solution.py:154
  244.6 108.8 %all-reduce.36.cloned.1.call-start = ((), (), s32[]{:S(2)}) async-start(), calls=%async_computation.5 | async-start | bytes 2097152 | tf_op jit(solution)/shard_map/psum | solution.py:154
  245.5 7.5 %copy-start.31 = (bf16[512,512]{1,0:T(8,128)(2,1)S(1)}, bf16[512,512]{1,0:T(8,128)(2,1)}, u32[]{:S(2)}) copy-start(bf16[512,512]{1,0:T(8,128)(2,1)} %copy-done.30) | copy-start | bytes 1572868
  247.0 34.2 %copy-start.9 = (f32[512,512]{1,0:T(8,128)S(1)}, f32[512,512]{1,0:T(8,128)}, u32[]{:S(2)}) copy-start(f32[512,512]{1,0:T(8,128)} %copy-done.8) | copy-start | bytes 3145732
  282.9 28.8 %copy-start.15 = (bf16[512,512]{1,0:T(8,128)(2,1)}, bf16[512,512]{1,0:T(8,128)(2,1)S(1)}, u32[]{:S(2)}) copy-start(bf16[512,512]{1,0:T(8,128)(2,1)S(1)} %fusion.67) | copy-start | bytes 1572868
  320.4 6.1 copy-start.16
  320.4 128.6 %all-reduce.38.cloned.1.call-start = ((), (), s32[]{:S(2)}) async-start(), calls=%async_computation.6 | async-start | bytes 2097152 | tf_op jit(solution)/shard_map/psum | solution.py:154
  323.4 30.1 %copy-start.92 = (f32[512]{0:T(512)S(1)}, f32[512]{0:T(512)}, u32[]{:S(2)}) copy-start(f32[512]{0:T(512)} %copy-done.91) | copy-start | bytes 6148
  327.5 29.4 %copy-start.61 = (bf16[128,512]{1,0:T(8,128)(2,1)S(1)}, bf16[128,512]{1,0:T(8,128)(2,1)}, u32[]{:S(2)}) copy-start(bf16[128,512]{1,0:T(8,128)(2,1)} %param.23) | copy-start | bytes 393220
  327.5 29.9 %copy-start.109 = (f32[2,2,64]{2,1,0:T(2,128)S(1)}, f32[2,2,64]{2,1,0:T(2,128)}, u32[]{:S(2)}) copy-start(f32[2,2,64]{2,1,0:T(2,128)} %copy-done.108) | copy-start | bytes 3076
  412.4 97.2 %all-reduce.40.cloned.1.call-start = ((), (), s32[]{:S(2)}) async-start(), calls=%async_computation.7 | async-start | bytes 2097152 | tf_op jit(solution)/shard_map/psum | solution.py:154
  417.9 31.2 %copy-start.21 = (f32[512,512]{1,0:T(8,128)S(1)}, f32[512,512]{1,0:T(8,128)}, u32[]{:S(2)}) copy-start(f32[512,512]{1,0:T(8,128)} %get-tuple-element.117) | copy-start | bytes 3145732
  454.6 262.3 %all-reduce.42.cloned.1.call-start = ((), (), s32[]{:S(2)}) async-start(), calls=%async_computation.8 | async-start | bytes 12582912 | tf_op jit(solution)/shard_map/psum | solution.py:267
  458.8 5.9 copy-start.118
  458.8 5.9 copy-start.119
  458.8 12.3 %copy-start.117 = (f32[512]{0:T(512)S(1)}, f32[512]{0:T(512)}, u32[]{:S(2)}) copy-start(f32[512]{0:T(512)} %get-tuple-element.82) | copy-start | bytes 6148
  458.8 12.3 %copy-start.123 = (f32[128]{0:T(128)S(1)}, f32[128]{0:T(128)}, u32[]{:S(2)}) copy-start(f32[128]{0:T(128)} %get-tuple-element.88) | copy-start | bytes 1540
  458.8 12.3 %copy-start.124 = (f32[128]{0:T(128)S(1)}, f32[128]{0:T(128)}, u32[]{:S(2)}) copy-start(f32[128]{0:T(128)} %get-tuple-element.89) | copy-start | bytes 1540
  (114 other events, 217.0 us)
Sparse Core Ops, SparseCore 0:
  17.1 38.8 all-reduce.25
  93.7 37.4 all-reduce.27
  159.9 32.8 all-reduce.29
  199.7 36.4 all-reduce.31
  244.7 36.4 all-reduce.33
  320.6 32.8 all-reduce.35
  412.5 36.5 all-reduce.37
  454.7 36.6 all-reduce.39
  498.2 218.6 all-reduce.41
where the time goes:
time: 744 us; the launch traced here: 733 us
  waiting for transfers between devices  395 us (53%)
  local copies, waits for them, and re-layouts  102 us (14%)
  blocking collectives  88.3 us (12%)
  other arithmetic  75.2 us (10%)
  matrix products  56 us (8%)
  between operations  16 us (2%)
    psum x1, waiting for transfers between devices, per_device(): lax.psum((gain_grads, early_in_grad, early_back_grad, qkv_grad, pos_grad,...  205 us
    psum x4, waiting for transfers between devices, add_branch(): return base_rows + factor * lax.psum(partial_value, 'tensor')  108 us
    psum x4, waiting for transfers between devices, add_gradient(): cotangent_sum, gain_total = lax.psum((cotangent_in, gain_piece), 'tensor')  81.7 us
    psum x1, blocking collectives, per_device(): lax.psum((gain_grads, early_in_grad, early_back_grad, qkv_grad, pos_grad,...  38.5 us
    dot_general x27, matrix products, matmul(): jnp.dot(first_factor, second_factor, preferred_element_type=jnp.float32)  33.1 us
    another operation x2, other arithmetic  32.2 us
    unnamed x287, local copies, waits for them, and re-layouts  23.3 us
    psum x1, blocking collectives, per_device(): mean_grad, var_grad = lax.psum((mean_grad, var_grad), 'dp')  22 us
  transfers between devices with their start and end apart: 9, of which 8 were waited for; matrix products, arithmetic and copies ran while one was open for 10% of the time, Pallas kernels for 0%

commit v1 on v0

--- a/solution.py
+++ b/solution.py
@@ -147,7 +147,7 @@
 
 
 def add_branch(base_rows, partial_value, factor):
-    return base_rows + factor * lax.psum(partial_value, "tensor")
+    return base_rows + factor * jnp.sum(lax.all_gather(partial_value, "tensor"), axis=0)
 
 
 def add_gradient(base_rows, cotangent_in, gain_piece):

time: 744 us -> 792 us (1.065)
  local copies, waits for them, and re-layouts: 102 us -> 143 us
  waiting for transfers between devices: 395 us -> 374 us
  other arithmetic: 75.2 us -> 92.2 us
  matrix products: 56 us -> 66.2 us
    psum x4 -> x0, waiting for transfers between devices: 108 us -> none  [add_branch(): return base_rows + factor * lax.psum(partial_value, 'tensor')]
    all_gather x0 -> x4, waiting for transfers between devices: none -> 98.8 us  [add_branch(): lax.all_gather(partial_value, 'tensor')]
    reduce_sum x0 -> x4, other arithmetic: none -> 14 us  [add_branch(): jnp.sum(lax.all_gather(partial_value, 'tensor'), axis=0)]
    unnamed x287 -> x271, local copies, waits for them, and re-layouts: 23.3 us -> 35.3 us
    psum x4, waiting for transfers between devices: 81.7 us -> 72.3 us  [add_gradient(): cotangent_sum, gain_total = lax.psum((cotangent_in, gain_piece), 'tensor')]
    reduce_sum x0 -> x4, local copies, waits for them, and re-layouts: none -> 7.92 us  [add_branch(): jnp.sum(lax.all_gather(partial_value, 'tensor'), axis=0)]
  transfers between devices with their start and end apart: 9 -> 9, of which waited for: 8 -> 7; matrix products, arithmetic and copies ran while one was open for 10% -> 11% of each run, Pallas kernels for 0% -> 0%
where the time goes in v1:
time: 792 us; the launch traced here: 781 us
  waiting for transfers between devices  374 us (47%)
  local copies, waits for them, and re-layouts  143 us (18%)
  other arithmetic  92.2 us (12%)
  blocking collectives  88.5 us (11%)
  matrix products  66.2 us (8%)
  between operations  15.7 us (2%)
    psum x1, waiting for transfers between devices, per_device(): lax.psum((gain_grads, early_in_grad, early_back_grad, qkv_grad, pos_grad,...  202 us
    all_gather x4, waiting for transfers between devices, add_branch(): lax.all_gather(partial_value, 'tensor')  98.8 us
    psum x4, waiting for transfers between devices, add_gradient(): cotangent_sum, gain_total = lax.psum((cotangent_in, gain_piece), 'tensor')  72.3 us
    psum x1, blocking collectives, per_device(): lax.psum((gain_grads, early_in_grad, early_back_grad, qkv_grad, pos_grad,...  38 us
    dot_general x27, matrix products, matmul(): jnp.dot(first_factor, second_factor, preferred_element_type=jnp.float32)  36.9 us
    unnamed x271, local copies, waits for them, and re-layouts  35.3 us
    another operation x2, other arithmetic  32.2 us
    psum x1, blocking collectives, per_device(): lax.psum((jnp.sum(mixed_rows, axis=(0, 1)), jnp.sum(mixed_rows * mixed_ro...  22 us
  transfers between devices with their start and end apart: 9, of which 7 were waited for; matrix products, arithmetic and copies ran while one was open for 11% of the time, Pallas kernels for 0%

profile of v1, /device:TPU:0, one launch (start us, length us, event | category | flops | bytes accessed | tf_op | source)
XLA Modules:
  0.0 780.6 jit_solution(9628108663287623607)
XLA Ops:
  14.4 31.0 %fusion.20 = (bf16[1023,256,1]{0,2,1:T(2,128)(2,1)S(1)}, bf16[1023,256,1]{0,2,1:T(2,128)(2,1)S(1)}) fusion(f32[1023]{0:T(1024)S(1)} %subtract_convert_fusion, f32[256]{0:T(256)S(1)} %multiply_exponential_fusion), kind=kLoop, calls=%fused_computation.49 | loop fusion | flops 785664 | bytes 1052668 | tf_op jit(solution)/shard_map/convert.3
  51.7 3.7 reduce_sum.379
  60.1 3.2 pad.50
  63.3 4.9 reshape.456
  68.3 4.9 slice.118
  73.2 6.5 reshape.457
  85.9 3.8 fusion.102
  95.9 35.4 %all-gather.11.cloned.1.call-done = f32[2048,512]{1,0:T(8,128)} async-done(((f32[512,512]{1,0:T(8,128)}), f32[2048,512]{1,0:T(8,128)}) %all-gather.11.cloned.1.call-update) | async-done | bytes 4194320 | tf_op jit(solution)/shard_map/all_gather | solution.py:150
  140.4 22.0 %all-reduce.13 = (f32[128]{0:T(128)}, f32[128]{0:T(128)}) all-reduce(f32[128]{0:T(128)} %get-tuple-element.135, f32[128]{0:T(128)S(1)} %get-tuple-element.134), channel_id=1, replica_groups=mesh['tensor'=4,'dp'=8] {'dp'}, use_global_device_ids=true, to_apply=%region_11.12 | all-reduce | flops 256 | bytes 2048 | tf_op jit(solution)/shard_map/psum | solution.py:201
  173.3 30.9 %all-gather.13.cloned.1.call-done = f32[2048,512]{1,0:T(8,128)} async-done(((f32[512,512]{1,0:T(8,128)}), f32[2048,512]{1,0:T(8,128)}) %all-gather.13.cloned.1.call-update) | async-done | bytes 4194320 | tf_op jit(solution)/shard_map/all_gather | solution.py:150
  204.3 3.7 reduce_sum.394
  218.9 32.5 %all-gather.15.cloned.1.call-done = f32[2048,512]{1,0:T(8,128)} async-done(((f32[512,512]{1,0:T(8,128)}), f32[2048,512]{1,0:T(8,128)}) %all-gather.15.cloned.1.call-update) | async-done | bytes 4194320 | tf_op jit(solution)/shard_map/all_gather | solution.py:150
  251.5 3.7 reduce_sum.400
  285.1 17.7 %all-reduce.22.cloned.1.call-done = f32[512,512]{0,1:T(8,128)} async-done(((f32[512,512]{0,1:T(8,128)}), f32[512,512]{0,1:T(8,128)}) %all-reduce.22.cloned.1.call-update) | async-done | bytes 1048592 | tf_op jit(solution)/shard_map/psum | solution.py:154
  308.4 22.0 %all-reduce.12 = (f32[128]{0:T(128)}, f32[128]{0:T(128)}) all-reduce(f32[128]{0:T(128)} %neg.55, f32[128]{0:T(128)} %multiply_multiply_fusion.5), channel_id=1, replica_groups=mesh['tensor'=4,'dp'=8] {'dp'}, use_global_device_ids=true, to_apply=%region_26.27 | all-reduce | flops 256 | bytes 2048 | tf_op jit(solution)/shard_map/psum | solution.py:225
  358.2 23.8 %all-reduce.24.cloned.1.call-done = f32[512,512]{0,1:T(8,128)} async-done(((f32[512,512]{0,1:T(8,128)}), f32[512,512]{0,1:T(8,128)}) %all-reduce.24.cloned.1.call-update) | async-done | bytes 1048592 | tf_op jit(solution)/shard_map/psum | solution.py:154
  382.0 3.2 fusion.92
  394.7 3.2 pad.53
  397.9 5.1 reshape.463
  403.0 4.9 slice.135
  407.9 6.5 reshape.464
  414.4 3.1 slice.136
  420.4 4.0 fusion.103
  437.3 7.1 reshape.465
  444.4 3.4 pad.57
  447.8 4.2 reshape.466
  452.1 3.3 fusion.12
  466.0 30.8 %all-reduce.26.cloned.1.call-done = f32[512,512]{0,1:T(8,128)} async-done(((f32[512,512]{0,1:T(8,128)}), f32[512,512]{0,1:T(8,128)}) %all-reduce.26.cloned.1.call-update) | async-done | bytes 1048592 | tf_op jit(solution)/shard_map/psum | solution.py:154
  507.7 5.9 fusion.106
  514.6 6.5 all-reduce.15
  521.2 38.0 %all-reduce.11 = (f32[5,512]{1,0:T(8,128)}, f32[2,2,64]{2,1,0:T(2,128)}, f32[31,128]{1,0:T(8,128)}, f32[128]{0:T(128)}, f32[128]{0:T(128)}) all-reduce(f32[5,512]{1,0:T(8,128)S(1)} %stack.27, f32[2,2,64]{2,1,0:T(2,128)S(1)} %pad_add_fusion, f32[31,128]{1,0:T(8,128)S(1)} %bitcast.243, ...), channel_id=1, replica_groups=mesh['tensor'=4,'dp'=8] {'dp'}, use_global_device_ids=true, to_apply=%region_50.51 | all-reduce | flops 7040 | bytes 56320 | tf_op jit(solution)/shard_map/psum | solution.py:267
  562.0 202.5 %all-reduce.30.cloned.1.call-done = (f32[512,512]{1,0:T(8,128)}, f32[512,512]{1,0:T(8,128)}, f32[512,3,128]{2,0,1:T(8,128)}, f32[512,128]{1,0:T(8,128)}, f32[128...) async-done(((f32[512,512]{1,0:T(8,128)}, f32[512,512]{1,0:T(8,128)}, f32[512,3,128]{2,0,1:T(8,128)}, ...) | async-done | bytes 6291472 | tf_op jit(solution)/shard_map/psum | solution.py:267
  (446 shorter events, 183.3 us)
Async XLA Ops:
  7.2 205.9 %copy-start = (bf16[512,512]{1,0:T(8,128)(2,1)S(1)}, bf16[512,512]{1,0:T(8,128)(2,1)}, u32[]{:S(2)}) copy-start(bf16[512,512]{1,0:T(8,128)(2,1)} %param.29) | copy-start | bytes 1572868
  7.2 3.9 copy-start.64
  7.2 44.5 %all-gather.9.cloned.1.call-start = ((), (), s32[]{:S(2)}) async-start(), calls=%async_computation.4 | async-start | bytes 5242880 | tf_op jit(solution)/shard_map/all_gather | solution.py:150
  8.7 3.9 copy-start.78
  14.1 117.2 %all-gather.11.cloned.1.call-start = ((), (), s32[]{:S(2)}) async-start(), calls=%async_computation.5 | async-start | bytes 5242880 | tf_op jit(solution)/shard_map/all_gather | solution.py:150
  14.2 37.0 %copy-start.102 = (f32[2,2,64]{2,1,0:T(2,128)}, f32[2,2,64]{2,1,0:T(2,128)S(1)}, u32[]{:S(2)}) copy-start(f32[2,2,64]{2,1,0:T(2,128)S(1)} %convert_element_type.243) | copy-start | bytes 3076
  48.7 6.7 copy-start.9
  93.9 110.3 %all-gather.13.cloned.1.call-start = ((), (), s32[]{:S(2)}) async-start(), calls=%async_computation.6 | async-start | bytes 5242880 | tf_op jit(solution)/shard_map/all_gather | solution.py:150
  163.7 9.6 %copy-start.103 = (f32[128]{0:T(128)}, f32[128]{0:T(128)S(1)}, u32[]{:S(2)}) copy-start(f32[128]{0:T(128)S(1)} %get-tuple-element.174) | copy-start | bytes 1540
  173.3 78.2 %all-gather.15.cloned.1.call-start = ((), (), s32[]{:S(2)}) async-start(), calls=%async_computation.7 | async-start | bytes 5242880 | tf_op jit(solution)/shard_map/all_gather | solution.py:150
  216.8 86.0 %all-reduce.22.cloned.1.call-start = ((), (), s32[]{:S(2)}) async-start(), calls=%async_computation | async-start | bytes 2097152 | tf_op jit(solution)/shard_map/psum | solution.py:154
  266.6 115.4 %all-reduce.24.cloned.1.call-start = ((), (), s32[]{:S(2)}) async-start(), calls=%async_computation.1 | async-start | bytes 2097152 | tf_op jit(solution)/shard_map/psum | solution.py:154
  267.8 6.9 copy-start.38
  275.5 27.3 %copy-start.8 = (bf16[512,512]{0,1:T(8,128)(2,1)S(1)}, bf16[512,512]{0,1:T(8,128)(2,1)}, u32[]{:S(2)}) copy-start(bf16[512,512]{0,1:T(8,128)(2,1)} %copy.111) | copy-start | bytes 1572868
  302.9 5.0 copy-start.117
  349.0 147.7 %all-reduce.26.cloned.1.call-start = ((), (), s32[]{:S(2)}) async-start(), calls=%async_computation.2 | async-start | bytes 2097152 | tf_op jit(solution)/shard_map/psum | solution.py:154
  351.7 30.3 %copy-start.5 = (f32[512,512]{0,1:T(8,128)S(1)}, f32[512,512]{0,1:T(8,128)}, u32[]{:S(2)}) copy-start(f32[512,512]{0,1:T(8,128)} %copy-done.4) | copy-start | bytes 3145732
  382.0 4.0 copy-start.57
  385.2 5.5 copy-start.10
  460.1 4.7 copy-start.70
  460.2 99.1 %all-reduce.28.cloned.1.call-start = ((), (), s32[]{:S(2)}) async-start(), calls=%async_computation.3 | async-start | bytes 2097152 | tf_op jit(solution)/shard_map/psum | solution.py:154
  466.0 32.7 %copy-start.63 = (bf16[512,512]{1,0:T(8,128)(2,1)S(1)}, bf16[512,512]{1,0:T(8,128)(2,1)}, u32[]{:S(2)}) copy-start(bf16[512,512]{1,0:T(8,128)(2,1)} %param.19) | copy-start | bytes 1572868
  502.2 262.2 %all-reduce.30.cloned.1.call-start = ((), (), s32[]{:S(2)}) async-start(), calls=%async_computation.8 | async-start | bytes 12582912 | tf_op jit(solution)/shard_map/psum | solution.py:267
  507.6 6.0 copy-start.34
  507.6 7.0 copy-start.115
  507.6 7.0 copy-start.116
  507.6 7.0 copy-start.106
  507.6 7.0 copy-start.107
  507.6 7.0 copy-start.108
  507.6 13.5 %copy-start.105 = (f32[512]{0:T(512)S(1)}, f32[512]{0:T(512)}, u32[]{:S(2)}) copy-start(f32[512]{0:T(512)} %get-tuple-element.128) | copy-start | bytes 6148
  507.6 13.6 %copy-start.112 = (f32[128]{0:T(128)S(1)}, f32[128]{0:T(128)}, u32[]{:S(2)}) copy-start(f32[128]{0:T(128)} %get-tuple-element.138) | copy-start | bytes 1540
  507.7 13.6 %copy-start.113 = (f32[128]{0:T(128)S(1)}, f32[128]{0:T(128)}, u32[]{:S(2)}) copy-start(f32[128]{0:T(128)} %get-tuple-element.139) | copy-start | bytes 1540
  (103 other events, 192.1 us)
Sparse Core Ops, SparseCore 0:
  14.2 37.1 all-gather.8
  94.0 37.1 all-gather.10
  173.4 30.7 all-gather.12
  216.9 34.4 all-gather.14
  266.7 36.0 all-reduce.21
  349.1 32.8 all-reduce.23
  460.3 36.4 all-reduce.25
  502.3 36.4 all-reduce.27
  545.7 218.6 all-reduce.29
